TPU v7x, 32 devices: a whole 2x2x4 slice. The times are simulated.
32 devices in a mesh: section: 2 (over x), space: 16 (over z, y, core).
Axes of the slice: x: 2, y: 2, z: 4, core: 2. Of those that a mesh axis runs over, the one named last changes fastest.
Arguments:
- acts: bfloat16 [2, 2, 2048, 1024], P('section', None, 'space'), may hold values from -6 to 6
- upstream: bfloat16 [2, 2048, 1024], P(None, 'space'), may hold values from -4 to 4
- weights: bfloat16 [2, 1024, 1024], P('section'), may hold values from -0.1875 to 0.1875
- neighbours: int32 [2048, 6], P('space'), may hold values from 0 to 2047, as said below
Outputs:
- input_grads: bfloat16 [2, 2, 2048, 1024], P('section', None, 'space')
- weight_grads: float32 [2, 1024, 1024], P('section', 'space')
Inputs may be any that keep to these rules, and one draw needn't show every extreme that they name: neighbours[i, k] is a node at most 32 positions from node i along the node order, taken cyclically over all 2048 nodes; the distance 32 is reached on both sides.
All inputs are finite; a program needn't handle non-finite values.
Results may differ from a plain program's by a relative error of at most 0.014.
Values may be sent and summed in bfloat16 or wider, within the bound.
A program may use at most 64 MiB of HBM per device.

v0:
```python
import jax
import jax.numpy as jnp
from jax import lax
from jax.sharding import PartitionSpec as P

K = 6
HALO = 32


def extended_2(block, sides, width):
    for axis, dim in sides:
        count = lax.axis_size(axis)
        forward = [(i, i + 1) for i in range(count - 1)]
        forward.append((count - 1, 0))
        backward = [(target, source) for source, target in forward]
        low = lax.ppermute(
            lax.slice_in_dim(block, block.shape[dim] - width, None, axis=dim), axis, forward
        )
        high = lax.ppermute(lax.slice_in_dim(block, 0, width, axis=dim), axis, backward)
        block = jnp.concatenate([low, block, high], axis=dim)
    return block


def shifted(value, axis, steps):
    count = lax.axis_size(axis)
    first, last = (max(0, -steps), min(count, count - steps))
    return lax.ppermute(value, axis, [(source, source + steps) for source in range(first, last)])


def shards(acts, upstream, weights, neighbours):
    section_count = lax.axis_size("section")
    section_id = lax.axis_index("section")
    shard = lax.axis_index("space")
    rows = neighbours.shape[0]
    width = weights.shape[2]
    micro = upstream.shape[0]
    total_nodes = rows * lax.axis_size("space")
    local_ids = jnp.mod(neighbours - shard * rows + HALO, total_nodes)
    flat_ids = local_ids.reshape(-1)
    weight = weights[0]
    inputs = acts[0]
    extended_all = extended_2(inputs, (("space", 1),), HALO)

    def products(extended, h_field, g_field, keep):
        picked = jnp.take(extended, local_ids, axis=0).astype(jnp.float32)
        z_field = (h_field.astype(jnp.float32) + jnp.mean(picked, axis=1)).astype(jnp.bfloat16)
        u_field = jnp.dot(z_field, weight, preferred_element_type=jnp.float32)
        sig = jax.nn.sigmoid(u_field)
        du_field = (g_field.astype(jnp.float32) * sig * (1.0 + u_field * (1.0 - sig))).astype(
            jnp.bfloat16
        )
        dz_field = lax.dot_general(
            du_field, weight, (((1,), (1,)), ((), ())), preferred_element_type=jnp.float32
        )
        keep = keep + lax.dot_general(
            z_field, du_field, (((0,), (0,)), ((), ())), preferred_element_type=jnp.float32
        )
        return (dz_field, keep)

    def tick(step, carry):
        received, grads, keep = carry
        batch = step - (section_count - 1 - section_id)
        valid = jnp.logical_and(batch >= 0, batch < micro)
        index = jnp.clip(batch, 0, micro - 1)
        h_field = lax.dynamic_index_in_dim(inputs, index, 0, False)
        g_field = jnp.where(
            section_id == section_count - 1,
            lax.dynamic_index_in_dim(upstream, index, 0, False),
            received,
        )
        extended = lax.dynamic_index_in_dim(extended_all, index, 0, False)

        def active(state):
            return products(extended, h_field, g_field, state)

        def resting(state):
            return (jnp.zeros((rows, width), jnp.float32), state)

        dz_field, keep = lax.cond(valid, active, resting, keep)
        share = dz_field * (1.0 / K)
        spread = (
            jnp.zeros((rows + 2 * HALO, width), jnp.float32)
            .at[flat_ids]
            .add(jnp.broadcast_to(share[:, None, :], (rows, K, width)).reshape(-1, width))
        )
        outgoing = jnp.concatenate([spread[:HALO], spread[rows + HALO :]], axis=0)
        returned = extended_2(outgoing.astype(jnp.bfloat16), (("space", 0),), HALO).astype(
            outgoing.dtype
        )
        own = spread[HALO : HALO + rows]
        own = own + jnp.pad(returned[:HALO], ((0, rows - HALO), (0, 0)))
        own = own + jnp.pad(returned[3 * HALO :], ((rows - HALO, 0), (0, 0)))
        d_input = (g_field.astype(jnp.float32) + dz_field + own).astype(jnp.bfloat16)
        updated = lax.dynamic_update_index_in_dim(grads, d_input, index, 0)
        grads = jnp.where(valid, updated, grads)
        received = shifted(d_input, "section", -1)
        return (received, grads, keep)

    keep_start = jnp.zeros((width, width), jnp.float32)
    start = (
        jnp.zeros((rows, width), jnp.bfloat16),
        jnp.zeros((micro, rows, width), jnp.bfloat16),
        keep_start,
    )
    received, grads, keep = lax.fori_loop(0, micro + section_count - 1, tick, start)
    weight_grad = lax.psum_scatter(keep, "space", scatter_dimension=0, tiled=True)
    return (grads[None], weight_grad[None])


def solution(mesh):
    in_specs = (
        P("section", None, "space", None),
        P(None, "space", None),
        P("section", None, None),
        P("space", None),
    )
    out_specs = (P("section", None, "space", None), P("section", "space", None))
    return jax.shard_map(shards, mesh=mesh, in_specs=in_specs, out_specs=out_specs, check_vma=False)
```

profile of v0, /device:TPU:0, one launch (start us, length us, event | category | flops | bytes accessed | tf_op | source)
XLA Modules:
  0.0 245.7 jit_solution(7214742011989282789)
XLA Ops:
  7.2 1.0 fusion.16
  8.7 5.1 %collective-permute-start.4 = (bf16[2,32,1024]{2,1,0:T(8,128)(2,1)S(1)}, bf16[2,32,1024]{2,1,0:T(8,128)(2,1)S(1)}, u32[]{:S(2)}, u32[]{:S(2)}) collective-permute-start(bf16[2,32,1024]{2,1,0:T(8,128)(2,1)S(1)} %get-tuple-element.385), channel_id=1, source_target_pairs={{1,0},{2,1},{3,2},{4,3},{5,4},{6,5},{7,6},{8,7},{9,8},{10,9},{11,1... | collective-permute-start | bytes 393224 | tf_op jit(solution)/shard_map/ppermute | solution.py:19
  14.7 1.7 collective-permute-done.3
  16.5 1.1 pad_maximum_fusion
  17.6 2.5 %broadcast_in_dim.68 = f32[1024,1024]{1,0:T(8,128)} broadcast(f32[]{:T(128)} %constant.158.clone.1), dimensions={} | broadcast | bytes 4194308 | tf_op jit(solution)/shard_map/broadcast_in_dim | solution.py:99
  21.0 149.4 %while.22 = (s32[]{:T(128)}, bf16[128,1024]{1,0:T(8,128)(2,1)S(1)}, bf16[2,128,1024]{2,1,0:T(8,128)(2,1)}, f32[1024,1024]{1,0:T(8,128)}, pred[]{:T(512)}, /*inde...) while((s32[]{:T(128)}, bf16[128,1024]{1,0:T(8,128)(2,1)S(1)}, ...), condition=%wide.region_5.6_spmd, body=%wide.region_0.5_spmd.sunk | while | flops 816130048 | bytes 87066752 | solution.py:105
  21.0 1.0 bitcast_select_fusion.3
  22.1 2.5 %broadcast_in_dim.74 = f32[128,6,1024]{2,1,0:T(8,128)} broadcast(f32[128,1024]{1,0:T(8,128)S(1)} %broadcast_multiply_fusion.2), dimensions={0,2} | broadcast | bytes 3670016 | tf_op jit(solution)/shard_map/while/body/eval_jaxpr/broadcast_in_dim | solution.py:84
  24.6 4.7 %reshape.76 = f32[768,1024]{1,0:T(8,128)} reshape(f32[128,6,1024]{2,1,0:T(8,128)} %broadcast_in_dim.74) | data formatting | bytes 6291456 | tf_op jit(solution)/shard_map/while/body/eval_jaxpr/reshape | solution.py:84
  29.3 10.5 %scatter_custom_fusion.5 = f32[192,1024]{1,0:T(8,128)S(1)} fusion(s32[768]{0:T(1024)S(1)} %fusion.27, f32[768,1024]{1,0:T(8,128)} %reshape.76, f32[]{:T(128)} %constant.158.clone.1..sunk), kind=kCustom, calls=%fused_computation.20.clone.1 | custom fusion | flops 786432 | bytes 786944 | tf_op jit(solution)/shard_map/while/body/eval_jaxpr/scatter-add | solution.py:84
  39.9 4.4 %collective-permute-start = (bf16[32,1024]{1,0:T(8,128)(2,1)S(1)}, bf16[32,1024]{1,0:T(8,128)(2,1)S(1)}, u32[]{:S(2)}, u32[]{:S(2)}) collective-permute-start(bf16[32,1024]{1,0:T(8,128)(2,1)S(1)} %get-tuple-element.466), channel_id=1, source_target_pairs={{1,0},{2,1},{3,2},{4,3},{5,4},{6,5},{7,6},{8,7},{9,8},{10,9},{11,1... | collective-permute-start | bytes 196616 | tf_op jit(solution)/shard_map/while/body/eval_jaxpr/ppermute | solution.py:19
  44.4 1.9 collective-permute-done
  46.3 4.5 %collective-permute-done.1 = bf16[32,1024]{1,0:T(8,128)(2,1)S(1)} collective-permute-done((bf16[32,1024]{1,0:T(8,128)(2,1)S(1)}, bf16[32,1024]{1,0:T(8,128)(2,1)S(1)}, u32[]{:S(2)}, u32[]{:S(2)}) %collective-permute-start.1) | collective-permute-done | bytes 65568 | tf_op jit(solution)/shard_map/while/body/eval_jaxpr/ppermute | solution.py:16
  50.8 1.9 fusion.29
  52.7 1.3 collective-permute-start.2
  54.0 19.2 %collective-permute-done.2 = bf16[128,1024]{1,0:T(8,128)(2,1)S(1)} collective-permute-done((bf16[128,1024]{1,0:T(8,128)(2,1)S(1)}, bf16[128,1024]{1,0:T(8,128)(2,1)S(1)}, u32[]{:S(2)}, u32[]{:S(2)}) %collective-permute-start.2) | collective-permute-done | bytes 262176 | tf_op jit(solution)/shard_map/while/body/eval_jaxpr/ppermute | solution.py:27
  73.1 1.0 bitcast_select_fusion.3
  74.1 13.0 %conditional.2 = (f32[128,1024]{1,0:T(8,128)S(1)}, f32[1024,1024]{1,0:T(8,128)}) conditional(s32[]{:T(128)} %convert_element_type.106, f32[1024,1024]{1,0:T(8,128)} %get-tuple-element.495, (bf16[128,1024]{1,0:T(8,128)(2,1)S(1)}, bf16[2,128,1024]{2,1,0:T(8,128)(2,1)}, s32[]{:T(128)}, s32[128,6]{1,0:T(8,128)S(1)}, bf16[2,192,1024]{2,1,0:T(8,128)(2,1)S(1)}, ...), branch_computations={%region_1.1_spmd, %region_2.3_spmd} | conditional | flops 811736832 | bytes 67922544 | solution.py:79
  74.4 2.8 %gather_fusion = bf16[768,1024]{1,0:T(8,128)(2,1)S(1)} fusion(bf16[192,1024]{1,0:T(8,128)(2,1)S(1)} %dynamic-slice_bitcast_fusion, s32[1024]{0:T(1024)S(1)} %pad_clamp_fusion), kind=kCustom, calls=%fused_computation | custom fusion | bytes 3148800 | tf_op jit(solution)/shard_map/while/body/eval_jaxpr/cond/branch_1_fun/jit(_take)/gather | solution.py:45
  77.2 1.6 reshape.48
  78.9 3.3 %convert_reduce_fusion = f32[128,1024]{1,0:T(8,128)S(1)} fusion(bf16[128,6,1024]{2,1,0:T(8,128)(2,1)} %reshape.48, pred[128,6]{1,0:T(8,128)(4,1)S(1)} %compare_and_fusion), kind=kLoop, calls=%fused_computation.2 | loop fusion | flops 2228224 | bytes 2097920 | tf_op jit(solution)/shard_map/while/body/eval_jaxpr/cond/branch_1_fun/reduce_sum | solution.py:46
  82.1 1.0 fusion
  83.7 1.5 convolution_add_fusion
  86.1 1.1 copy-done.1
  87.2 2.5 %broadcast_in_dim.74 = f32[128,6,1024]{2,1,0:T(8,128)} broadcast(f32[128,1024]{1,0:T(8,128)S(1)} %broadcast_multiply_fusion.2), dimensions={0,2} | broadcast | bytes 3670016 | tf_op jit(solution)/shard_map/while/body/eval_jaxpr/broadcast_in_dim | solution.py:84
  89.7 4.7 %reshape.76 = f32[768,1024]{1,0:T(8,128)} reshape(f32[128,6,1024]{2,1,0:T(8,128)} %broadcast_in_dim.74) | data formatting | bytes 6291456 | tf_op jit(solution)/shard_map/while/body/eval_jaxpr/reshape | solution.py:84
  94.4 10.5 %scatter_custom_fusion.5 = f32[192,1024]{1,0:T(8,128)S(1)} fusion(s32[768]{0:T(1024)S(1)} %fusion.27, f32[768,1024]{1,0:T(8,128)} %reshape.76, f32[]{:T(128)} %constant.158.clone.1..sunk), kind=kCustom, calls=%fused_computation.20.clone.1 | custom fusion | flops 786432 | bytes 786944 | tf_op jit(solution)/shard_map/while/body/eval_jaxpr/scatter-add | solution.py:84
  105.6 1.4 collective-permute-done
  107.0 4.5 %collective-permute-done.1 = bf16[32,1024]{1,0:T(8,128)(2,1)S(1)} collective-permute-done((bf16[32,1024]{1,0:T(8,128)(2,1)S(1)}, bf16[32,1024]{1,0:T(8,128)(2,1)S(1)}, u32[]{:S(2)}, u32[]{:S(2)}) %collective-permute-start.1) | collective-permute-done | bytes 65568 | tf_op jit(solution)/shard_map/while/body/eval_jaxpr/ppermute | solution.py:16
  111.6 1.9 fusion.29
  113.5 1.3 collective-permute-start.2
  114.8 7.0 %collective-permute-done.2 = bf16[128,1024]{1,0:T(8,128)(2,1)S(1)} collective-permute-done((bf16[128,1024]{1,0:T(8,128)(2,1)S(1)}, bf16[128,1024]{1,0:T(8,128)(2,1)S(1)}, u32[]{:S(2)}, u32[]{:S(2)}) %collective-permute-start.2) | collective-permute-done | bytes 262176 | tf_op jit(solution)/shard_map/while/body/eval_jaxpr/ppermute | solution.py:27
  122.7 13.0 %conditional.2 = (f32[128,1024]{1,0:T(8,128)S(1)}, f32[1024,1024]{1,0:T(8,128)}) conditional(s32[]{:T(128)} %convert_element_type.106, f32[1024,1024]{1,0:T(8,128)} %get-tuple-element.495, (bf16[128,1024]{1,0:T(8,128)(2,1)S(1)}, bf16[2,128,1024]{2,1,0:T(8,128)(2,1)}, s32[]{:T(128)}, s32[128,6]{1,0:T(8,128)S(1)}, bf16[2,192,1024]{2,1,0:T(8,128)(2,1)S(1)}, ...), branch_computations={%region_1.1_spmd, %region_2.3_spmd} | conditional | flops 811736832 | bytes 67922544 | solution.py:79
  123.0 2.8 %gather_fusion = bf16[768,1024]{1,0:T(8,128)(2,1)S(1)} fusion(bf16[192,1024]{1,0:T(8,128)(2,1)S(1)} %dynamic-slice_bitcast_fusion, s32[1024]{0:T(1024)S(1)} %pad_clamp_fusion), kind=kCustom, calls=%fused_computation | custom fusion | bytes 3148800 | tf_op jit(solution)/shard_map/while/body/eval_jaxpr/cond/branch_1_fun/jit(_take)/gather | solution.py:45
  125.8 1.6 reshape.48
  127.4 3.3 %convert_reduce_fusion = f32[128,1024]{1,0:T(8,128)S(1)} fusion(bf16[128,6,1024]{2,1,0:T(8,128)(2,1)} %reshape.48, pred[128,6]{1,0:T(8,128)(4,1)S(1)} %compare_and_fusion), kind=kLoop, calls=%fused_computation.2 | loop fusion | flops 2228224 | bytes 2097920 | tf_op jit(solution)/shard_map/while/body/eval_jaxpr/cond/branch_1_fun/reduce_sum | solution.py:46
  130.7 1.0 fusion
  132.2 1.6 convolution_add_fusion
  134.7 1.1 copy-done.1
  135.8 2.5 %broadcast_in_dim.74 = f32[128,6,1024]{2,1,0:T(8,128)} broadcast(f32[128,1024]{1,0:T(8,128)S(1)} %broadcast_multiply_fusion.2), dimensions={0,2} | broadcast | bytes 3670016 | tf_op jit(solution)/shard_map/while/body/eval_jaxpr/broadcast_in_dim | solution.py:84
  138.3 4.7 %reshape.76 = f32[768,1024]{1,0:T(8,128)} reshape(f32[128,6,1024]{2,1,0:T(8,128)} %broadcast_in_dim.74) | data formatting | bytes 6291456 | tf_op jit(solution)/shard_map/while/body/eval_jaxpr/reshape | solution.py:84
  143.0 10.5 %scatter_custom_fusion.5 = f32[192,1024]{1,0:T(8,128)S(1)} fusion(s32[768]{0:T(1024)S(1)} %fusion.27, f32[768,1024]{1,0:T(8,128)} %reshape.76, f32[]{:T(128)} %constant.158.clone.1..sunk), kind=kCustom, calls=%fused_computation.20.clone.1 | custom fusion | flops 786432 | bytes 786944 | tf_op jit(solution)/shard_map/while/body/eval_jaxpr/scatter-add | solution.py:84
  154.2 1.4 collective-permute-done
  155.6 4.5 %collective-permute-done.1 = bf16[32,1024]{1,0:T(8,128)(2,1)S(1)} collective-permute-done((bf16[32,1024]{1,0:T(8,128)(2,1)S(1)}, bf16[32,1024]{1,0:T(8,128)(2,1)S(1)}, u32[]{:S(2)}, u32[]{:S(2)}) %collective-permute-start.1) | collective-permute-done | bytes 65568 | tf_op jit(solution)/shard_map/while/body/eval_jaxpr/ppermute | solution.py:16
  160.2 1.9 fusion.29
  162.1 1.3 collective-permute-start.2
  163.4 7.0 %collective-permute-done.2 = bf16[128,1024]{1,0:T(8,128)(2,1)S(1)} collective-permute-done((bf16[128,1024]{1,0:T(8,128)(2,1)S(1)}, bf16[128,1024]{1,0:T(8,128)(2,1)S(1)}, u32[]{:S(2)}, u32[]{:S(2)}) %collective-permute-start.2) | collective-permute-done | bytes 262176 | tf_op jit(solution)/shard_map/while/body/eval_jaxpr/ppermute | solution.py:27
  170.3 68.5 %reduce-scatter.2.cloned.1.call-done = f32[64,1024]{1,0:T(8,128)} async-done(((f32[1024,1024]{1,0:T(8,128)}), f32[64,1024]{1,0:T(8,128)}) %reduce-scatter.2.cloned.1.call-update) | async-done | bytes 262160 | tf_op jit(solution)/shard_map/reduce_scatter | solution.py:106
  (61 shorter events, 8.2 us)
Async XLA Ops:
  7.2 231.7 %reduce-scatter.2.cloned.1.call-start = ((), (), s32[]{:S(2)}) async-start(), calls=%async_computation.1 | async-start | bytes 4456448 | tf_op jit(solution)/shard_map/reduce_scatter | solution.py:106
  8.2 8.3 %collective-permute-start.3 = (bf16[2,32,1024]{2,1,0:T(8,128)(2,1)S(1)}, bf16[2,32,1024]{2,1,0:T(8,128)(2,1)S(1)}, u32[]{:S(2)}, u32[]{:S(2)}) collective-permute-start(bf16[2,32,1024]{2,1,0:T(8,128)(2,1)S(1)} %get-tuple-element.384), channel_id=1, source_target_pairs={{0,1},{1,2},{2,3},{3,4},{4,5},{5,6},{6,7},{7,8},{8,9},{9,10},{10,1... | collective-permute-start | bytes 393224 | tf_op jit(solution)/shard_map/ppermute | solution.py:16
  8.7 7.8 %collective-permute-start.4 = (bf16[2,32,1024]{2,1,0:T(8,128)(2,1)S(1)}, bf16[2,32,1024]{2,1,0:T(8,128)(2,1)S(1)}, u32[]{:S(2)}, u32[]{:S(2)}) collective-permute-start(bf16[2,32,1024]{2,1,0:T(8,128)(2,1)S(1)} %get-tuple-element.385), channel_id=1, source_target_pairs={{1,0},{2,1},{3,2},{4,3},{5,4},{6,5},{7,6},{8,7},{9,8},{10,9},{11,1... | collective-permute-start | bytes 393224 | tf_op jit(solution)/shard_map/ppermute | solution.py:19
  17.6 3.4 %copy-start.3 = (pred[128]{0:T(512)(128)(4,1)S(1)}, pred[128]{0:T(512)(128)(4,1)}, u32[]{:S(2)}) copy-start(pred[128]{0:T(512)(128)(4,1)} %constant.154.clone.1) | copy-start | bytes 388
  39.9 6.4 %collective-permute-start = (bf16[32,1024]{1,0:T(8,128)(2,1)S(1)}, bf16[32,1024]{1,0:T(8,128)(2,1)S(1)}, u32[]{:S(2)}, u32[]{:S(2)}) collective-permute-start(bf16[32,1024]{1,0:T(8,128)(2,1)S(1)} %get-tuple-element.466), channel_id=1, source_target_pairs={{1,0},{2,1},{3,2},{4,3},{5,4},{6,5},{7,6},{8,7},{9,8},{10,9},{11,1... | collective-permute-start | bytes 196616 | tf_op jit(solution)/shard_map/while/body/eval_jaxpr/ppermute | solution.py:19
  44.4 6.4 %collective-permute-start.1 = (bf16[32,1024]{1,0:T(8,128)(2,1)S(1)}, bf16[32,1024]{1,0:T(8,128)(2,1)S(1)}, u32[]{:S(2)}, u32[]{:S(2)}) collective-permute-start(bf16[32,1024]{1,0:T(8,128)(2,1)S(1)} %get-tuple-element.467), channel_id=1, source_target_pairs={{0,1},{1,2},{2,3},{3,4},{4,5},{5,6},{6,7},{7,8},{8,9},{9,10},{10,1... | collective-permute-start | bytes 196616 | tf_op jit(solution)/shard_map/while/body/eval_jaxpr/ppermute | solution.py:16
  52.7 20.4 %collective-permute-start.2 = (bf16[128,1024]{1,0:T(8,128)(2,1)S(1)}, bf16[128,1024]{1,0:T(8,128)(2,1)S(1)}, u32[]{:S(2)}, u32[]{:S(2)}) collective-permute-start(bf16[128,1024]{1,0:T(8,128)(2,1)S(1)} %get-tuple-element.468), channel_id=1, source_target_pairs={{16,0},{17,1},{18,2},{19,3},{20,4},{21,5},{22,6},{23,7},{24,8},{25... | collective-permute-start | bytes 786440 | tf_op jit(solution)/shard_map/while/body/eval_jaxpr/ppermute | solution.py:27
  78.8 4.4 %copy-start.2 = (bf16[1024,1024]{1,0:T(8,128)(2,1)S(1)}, bf16[1024,1024]{1,0:T(8,128)(2,1)}, u32[]{:S(2)}) copy-start(bf16[1024,1024]{1,0:T(8,128)(2,1)} %get-tuple-element.321) | copy-start | bytes 6291460 | tf_op jit(solution)/shard_map/while/body/eval_jaxpr/cond
  78.9 4.8 %copy-start = (f32[1024,1024]{1,0:T(8,128)S(1)}, f32[1024,1024]{1,0:T(8,128)}, u32[]{:S(2)}) copy-start(f32[1024,1024]{1,0:T(8,128)} %get-tuple-element.322) | copy-start | bytes 12582916 | tf_op jit(solution)/shard_map/while/body/eval_jaxpr/cond
  85.2 2.0 copy-start.1
  105.0 2.0 collective-permute-start
  105.1 6.4 %collective-permute-start.1 = (bf16[32,1024]{1,0:T(8,128)(2,1)S(1)}, bf16[32,1024]{1,0:T(8,128)(2,1)S(1)}, u32[]{:S(2)}, u32[]{:S(2)}) collective-permute-start(bf16[32,1024]{1,0:T(8,128)(2,1)S(1)} %get-tuple-element.467), channel_id=1, source_target_pairs={{0,1},{1,2},{2,3},{3,4},{4,5},{5,6},{6,7},{7,8},{8,9},{9,10},{10,1... | collective-permute-start | bytes 196616 | tf_op jit(solution)/shard_map/while/body/eval_jaxpr/ppermute | solution.py:16
  113.5 8.3 %collective-permute-start.2 = (bf16[128,1024]{1,0:T(8,128)(2,1)S(1)}, bf16[128,1024]{1,0:T(8,128)(2,1)S(1)}, u32[]{:S(2)}, u32[]{:S(2)}) collective-permute-start(bf16[128,1024]{1,0:T(8,128)(2,1)S(1)} %get-tuple-element.468), channel_id=1, source_target_pairs={{16,0},{17,1},{18,2},{19,3},{20,4},{21,5},{22,6},{23,7},{24,8},{25... | collective-permute-start | bytes 786440 | tf_op jit(solution)/shard_map/while/body/eval_jaxpr/ppermute | solution.py:27
  127.4 4.4 %copy-start.2 = (bf16[1024,1024]{1,0:T(8,128)(2,1)S(1)}, bf16[1024,1024]{1,0:T(8,128)(2,1)}, u32[]{:S(2)}) copy-start(bf16[1024,1024]{1,0:T(8,128)(2,1)} %get-tuple-element.321) | copy-start | bytes 6291460 | tf_op jit(solution)/shard_map/while/body/eval_jaxpr/cond
  127.4 4.8 %copy-start = (f32[1024,1024]{1,0:T(8,128)S(1)}, f32[1024,1024]{1,0:T(8,128)}, u32[]{:S(2)}) copy-start(f32[1024,1024]{1,0:T(8,128)} %get-tuple-element.322) | copy-start | bytes 12582916 | tf_op jit(solution)/shard_map/while/body/eval_jaxpr/cond
  133.8 2.0 copy-start.1
  153.6 2.0 collective-permute-start
  153.7 6.4 %collective-permute-start.1 = (bf16[32,1024]{1,0:T(8,128)(2,1)S(1)}, bf16[32,1024]{1,0:T(8,128)(2,1)S(1)}, u32[]{:S(2)}, u32[]{:S(2)}) collective-permute-start(bf16[32,1024]{1,0:T(8,128)(2,1)S(1)} %get-tuple-element.467), channel_id=1, source_target_pairs={{0,1},{1,2},{2,3},{3,4},{4,5},{5,6},{6,7},{7,8},{8,9},{9,10},{10,1... | collective-permute-start | bytes 196616 | tf_op jit(solution)/shard_map/while/body/eval_jaxpr/ppermute | solution.py:16
  162.1 8.3 %collective-permute-start.2 = (bf16[128,1024]{1,0:T(8,128)(2,1)S(1)}, bf16[128,1024]{1,0:T(8,128)(2,1)S(1)}, u32[]{:S(2)}, u32[]{:S(2)}) collective-permute-start(bf16[128,1024]{1,0:T(8,128)(2,1)S(1)} %get-tuple-element.468), channel_id=1, source_target_pairs={{16,0},{17,1},{18,2},{19,3},{20,4},{21,5},{22,6},{23,7},{24,8},{25... | collective-permute-start | bytes 786440 | tf_op jit(solution)/shard_map/while/body/eval_jaxpr/ppermute | solution.py:27
Sparse Core Ops, SparseCore 0:
  170.5 68.3 reduce-scatter.1
where the time goes:
time: 246 us
  waiting for transfers between devices  122 us (50%)
  other arithmetic  51 us (21%)
  local copies, waits for them, and re-layouts  37.8 us (15%)
  starting transfers between devices  15 us (6%)
  between operations  14.1 us (6%)
  matrix products  5.69 us (2%)
    reduce_scatter x1, waiting for transfers between devices, shards(): lax.psum_scatter(keep, 'space', scatter_dimension=0, tiled=True)  68.5 us
    ppermute x3, waiting for transfers between devices, shifted(): lax.ppermute(value, axis, [(source, source + steps) for source in range(f...  33.1 us
    scatter-add x3, other arithmetic, tick(): spread = jnp.zeros((rows + 2 * HALO, width), jnp.float32).at[flat_ids].ad...  31.5 us
    ppermute x4, waiting for transfers between devices, extended_2(): lax.ppermute(lax.slice_in_dim(block, block.shape[dim] - width, None, axis...  15.3 us
    reshape x3, local copies, waits for them, and re-layouts, tick(): jnp.broadcast_to(share[:, None, :], (rows, K, width)).reshape(-1, width)  14.2 us
    ppermute x4, starting transfers between devices, extended_2(): lax.ppermute(lax.slice_in_dim(block, 0, width, axis=dim), axis, backward)  9.62 us
    gather x4, local copies, waits for them, and re-layouts, products(): picked = jnp.take(extended, local_ids, axis=0).astype(jnp.float32)  8.89 us
    broadcast_in_dim x3, local copies, waits for them, and re-layouts, tick(): jnp.broadcast_to(share[:, None, :], (rows, K, width)).reshape(-1, width)  7.4 us
  transfers between devices with their start and end apart: 12, of which 11 were waited for; matrix products, arithmetic and copies ran while one was open for 0% of the time, Pallas kernels for 0%

commit v1 on v0

v1 whole, which is shorter than its diff:
```python
import functools

import jax
import jax.numpy as jnp
from jax import lax
from jax.experimental import pallas as pl
from jax.experimental.pallas import tpu as pltpu
from jax.sharding import PartitionSpec as P

K = 6
HALO = 32
CHUNK = 256
MESH = pl.DeviceIdType.MESH
F32 = jnp.float32
BF16 = jnp.bfloat16


def radices_of(count):
    found = []
    for _ in range(2):
        if count % 2 == 0:
            found.append(2)
            count //= 2
    while count > 1:
        factor = next(f for f in (2, 3, 5, 7, count) if count % f == 0)
        found.append(factor)
        count //= factor
    return tuple(found)


def position(piece, radices):
    left = 1
    for r in radices:
        left *= r
    place = 0
    for r in radices:
        left //= r
        place += (piece % r) * left
        piece //= r
    return place


def kernel(sections, count, radices, chunk, nbr, acts, ups_hbm, w_hbm, out, wgrad, *scratch):
    (w, ups, acts_lo, acts_hi, nbr_lo, nbr_hi, z, zt, fac, g_in, g_out, du, du_lo, du_hi, e,
     load_sem, acts_send, acts_recv, nbr_send, nbr_recv, g_send, g_recv, du_send, du_recv,
     rs_send, rs_recv, *rs) = scratch
    stages = len(radices)
    parts, landed = rs[:stages], rs[stages:]
    micro, rows, width = acts.shape
    chunks = width // chunk
    span = rows + 2 * HALO
    s = lax.axis_index("section")
    me = lax.axis_index("space")
    right, left = lax.rem(me + 1, count), lax.rem(me + count - 1, count)
    top = s == sections - 1

    strides, digits, stride = [], [], 1
    for r in radices:
        strides.append(stride)
        digits.append(lax.rem(lax.div(me, stride), r))
        stride *= r

    def peer(t, j):
        digit = lax.rem(digits[t] + j, radices[t])
        return digit, me + (digit - digits[t]) * strides[t]

    loads = [pltpu.make_async_copy(w_hbm, w, load_sem.at[0]),
             pltpu.make_async_copy(ups_hbm, ups, load_sem.at[1])]
    for copy in loads:
        copy.start()

    barrier = pltpu.get_barrier_semaphore()
    partners = [left, right] + [peer(t, j)[1] for t in range(stages) for j in range(1, radices[t])]
    for partner in partners:
        pl.semaphore_signal(barrier, inc=1, device_id=(s, partner), device_id_type=MESH)

    @pl.when(s > 0)
    def _():
        pl.semaphore_signal(barrier, inc=1, device_id=(s - 1, me), device_id_type=MESH)

    @pl.when(s < sections - 1)
    def _():
        pl.semaphore_signal(barrier, inc=1, device_id=(s + 1, me), device_id_type=MESH)

    layers = jnp.where(s > 0, 1, 0) + jnp.where(s < sections - 1, 1, 0)
    pl.semaphore_wait(barrier, len(partners) + layers)

    def remote(src, dst, send, recv, where):
        return pltpu.make_async_remote_copy(
            src_ref=src, dst_ref=dst, send_sem=send, recv_sem=recv, device_id=where,
            device_id_type=MESH)

    first, last = pl.ds(0, HALO), pl.ds(rows - HALO, HALO)
    halos = [
        remote(acts.at[:, last], acts_lo, acts_send.at[0], acts_recv.at[0], (s, right)),
        remote(acts.at[:, first], acts_hi, acts_send.at[1], acts_recv.at[1], (s, left)),
        remote(nbr.at[last], nbr_lo, nbr_send.at[0], nbr_recv.at[0], (s, right)),
        remote(nbr.at[first], nbr_hi, nbr_send.at[1], nbr_recv.at[1], (s, left)),
    ]
    for copy in halos:
        copy.start()

    total = rows * count

    def counts(ids, shift, lanes):
        local = ids - me * rows + shift
        local = jnp.where(local < 0, local + total, local)
        local = jnp.where(local >= total, local - total, local)
        places = lax.broadcasted_iota(jnp.int32, (ids.shape[0], lanes), 1)
        found = jnp.zeros(places.shape, F32)
        for k in range(K):
            found = found + jnp.where(local[:, k:k + 1] == places, 1.0, 0.0)
        return found.astype(BF16)

    gather = counts(nbr[...], HALO, span)
    own = counts(nbr[...], 0, rows)

    for copy in halos:
        copy.wait_recv()
    scatter = jnp.concatenate(
        [counts(nbr_lo[...], 0, rows), own, counts(nbr_hi[...], 0, rows)], axis=0
    ).astype(F32).T.astype(BF16)

    for m in range(micro):
        field = jnp.concatenate([acts_lo[m], acts[m], acts_hi[m]], axis=0)
        agg = jnp.dot(gather, field, preferred_element_type=F32) * (1.0 / K)
        z[m * rows:(m + 1) * rows] = (acts[m].astype(F32) + agg).astype(BF16)
    for copy in loads:
        copy.wait()

    def columns(c):
        return slice(c * chunk, (c + 1) * chunk)

    def factor(c):
        u = jnp.dot(z[...], w[:, columns(c)], preferred_element_type=F32)
        sig = jax.nn.sigmoid(u)
        return sig * (1.0 + u * (1.0 - sig))

    def turn():
        zt[...] = z[...].astype(F32).T.astype(BF16)

    def du_copies(c):
        return [
            remote(du.at[c, :, last], du_lo.at[c], du_send.at[2 * c], du_recv.at[2 * c], (s, right)),
            remote(du.at[c, :, first], du_hi.at[c], du_send.at[2 * c + 1], du_recv.at[2 * c + 1],
                   (s, left)),
        ]

    def put_du(c, value):
        value = value.astype(BF16)
        du[c] = value.reshape(micro, rows, chunk)
        for copy in du_copies(c):
            copy.start()

    def mix(c):
        for copy in du_copies(c):
            copy.wait_recv()
        for m in range(micro):
            field = jnp.concatenate([du_lo[c, m], du[c, m], du_hi[c, m]], axis=0)
            spread = jnp.dot(scatter, field, preferred_element_type=F32) * (1.0 / K)
            e[m * rows:(m + 1) * rows, columns(c)] = (du[c, m].astype(F32) + spread).astype(BF16)

    def cotangent(c, g):
        value = g.astype(F32) + lax.dot_general(
            e[...], w[columns(c), :], (((1,), (1,)), ((), ())), preferred_element_type=F32)
        value = value.astype(BF16)
        out[:, columns(c)] = value
        return value

    def rs_copies(t, c):
        groups = parts[t].shape[1] // radices[t]
        base = sum(r - 1 for r in radices[:t]) * chunks + c * (radices[t] - 1)
        made = []
        for j in range(1, radices[t]):
            digit, partner = peer(t, j)
            made.append(remote(
                parts[t].at[c, pl.ds(digit * groups, groups)], landed[t].at[c, j - 1],
                rs_send.at[base + j - 1], rs_recv.at[base + j - 1], (s, partner)))
        return made

    def rs_start(t, c):
        for copy in rs_copies(t, c):
            copy.start()

    def weight_part(c):
        found = jnp.dot(zt[...], du[c].reshape(micro * rows, chunk), preferred_element_type=F32)
        found = found.astype(BF16)
        deep = width // count
        for piece in range(count):
            parts[0][c, position(piece, radices)] = found[piece * deep:(piece + 1) * deep]
        rs_start(0, c)

    def rs_step(t, c):
        for copy in rs_copies(t, c):
            copy.wait_recv()
        groups = parts[t].shape[1] // radices[t]
        value = parts[t][c, pl.ds(digits[t] * groups, groups)].astype(F32)
        for j in range(radices[t] - 1):
            value = value + landed[t][c, j].astype(F32)
        if t == stages - 1:
            wgrad[:, columns(c)] = value[0]
        else:
            parts[t + 1][c] = value.astype(BF16)
            rs_start(t + 1, c)

    def rs_wave(step):
        for t in reversed(range(stages)):
            if 0 <= step - t < chunks:
                rs_step(t, step - t)

    def g_copy(c):
        return remote(g_out.at[c], g_in.at[c], g_send.at[c], g_recv.at[c], (s - 1, me))

    @pl.when(top)
    def _():
        for c in range(chunks):
            put_du(c, ups[:, columns(c)].astype(F32) * factor(c))
        turn()
        for c in range(chunks):
            weight_part(c)
        for c in range(chunks):
            mix(c)
        for c in range(chunks):
            g_out[c] = cotangent(c, ups[:, columns(c)])
            if sections > 1:
                g_copy(c).start()
        for step in range(chunks + stages - 1):
            rs_wave(step)
        if sections > 1:
            for c in range(chunks):
                g_copy(c).wait_send()

    if sections > 1:
        @pl.when(jnp.logical_not(top))
        def _():
            for c in range(chunks):
                fac[:, columns(c)] = factor(c)
            turn()
            for c in range(chunks):
                g_copy(c).wait_recv()
                put_du(c, g_in[c].astype(F32) * fac[:, columns(c)])
                weight_part(c)
                if c:
                    rs_wave(c - 1)
            rs_wave(chunks - 1)
            for c in range(chunks):
                mix(c)
            for c in range(chunks):
                g_out[c] = cotangent(c, g_in[c])

                @pl.when(s > 0)
                def _():
                    g_copy(c).start()
            for step in range(chunks, chunks + stages - 1):
                rs_wave(step)

            @pl.when(s > 0)
            def _():
                for c in range(chunks):
                    g_copy(c).wait_send()

    for copy in halos:
        copy.wait_send()
    for c in range(chunks):
        for copy in du_copies(c):
            copy.wait_send()
        for t in range(stages):
            for copy in rs_copies(t, c):
                copy.wait_send()


def shards(sections, count, acts, upstream, weights, neighbours):
    micro, rows, width = upstream.shape
    chunk = min(CHUNK, width)
    chunks = width // chunk
    radices = radices_of(count)
    held, parts, landed = count, [], []
    deep = width // count
    for r in radices:
        parts.append(pltpu.VMEM((chunks, held, deep, chunk), BF16))
        held //= r
        landed.append(pltpu.VMEM((chunks, r - 1, held, deep, chunk), BF16))
    flights = sum(r - 1 for r in radices) * chunks
    dma = pltpu.SemaphoreType.DMA
    tall = micro * rows
    scratch = [
        pltpu.VMEM((width, width), BF16),
        pltpu.VMEM((tall, width), BF16),
        pltpu.VMEM((micro, HALO, width), BF16),
        pltpu.VMEM((micro, HALO, width), BF16),
        pltpu.VMEM((HALO, K), jnp.int32),
        pltpu.VMEM((HALO, K), jnp.int32),
        pltpu.VMEM((tall, width), BF16),
        pltpu.VMEM((width, tall), BF16),
        pltpu.VMEM((tall, width), F32),
        pltpu.VMEM((chunks, tall, chunk), BF16),
        pltpu.VMEM((chunks, tall, chunk), BF16),
        pltpu.VMEM((chunks, micro, rows, chunk), BF16),
        pltpu.VMEM((chunks, micro, HALO, chunk), BF16),
        pltpu.VMEM((chunks, micro, HALO, chunk), BF16),
        pltpu.VMEM((tall, width), BF16),
        dma((2,)), dma((2,)), dma((2,)), dma((2,)), dma((2,)), dma((chunks,)), dma((chunks,)),
        dma((2 * chunks,)), dma((2 * chunks,)), dma((flights,)), dma((flights,)),
    ] + parts + landed
    vmem = pl.BlockSpec(memory_space=pltpu.VMEM)
    grads, weight_grad = pl.pallas_call(
        functools.partial(kernel, sections, count, radices, chunk),
        out_shape=(
            jax.ShapeDtypeStruct((tall, width), BF16),
            jax.ShapeDtypeStruct((deep, width), F32),
        ),
        in_specs=[vmem, vmem, pl.BlockSpec(memory_space=pl.ANY), pl.BlockSpec(memory_space=pl.ANY)],
        out_specs=(vmem, vmem),
        scratch_shapes=scratch,
        compiler_params=pltpu.CompilerParams(
            collective_id=0, has_side_effects=True, vmem_limit_bytes=48 * 1024 * 1024),
    )(neighbours, acts[0], upstream.reshape(tall, width), weights[0])
    return grads.reshape(1, micro, rows, width), weight_grad[None]


def solution(mesh):
    in_specs = (
        P("section", None, "space", None),
        P(None, "space", None),
        P("section", None, None),
        P("space", None),
    )
    out_specs = (P("section", None, "space", None), P("section", "space", None))
    body = functools.partial(shards, mesh.shape["section"], mesh.shape["space"])
    return jax.shard_map(
        body, mesh=mesh, in_specs=in_specs, out_specs=out_specs, check_vma=False)
```

time: 246 us -> 58 us (0.24)
  waiting for transfers between devices: 122 us -> 0 us
  Pallas kernels: 0 us -> 51.1 us
  other arithmetic: 51 us -> 0 us
  local copies, waits for them, and re-layouts: 37.8 us -> 5.96 us
  starting transfers between devices: 15 us -> 0 us
  between operations: 14.1 us -> 0.65 us
  matrix products: 5.69 us -> 0 us
    reduce_scatter x1 -> x0, waiting for transfers between devices: 68.5 us -> none  [shards(): lax.psum_scatter(keep, 'space', scatter_dimension=0, tiled=True)]
    ppermute x11 -> x0, waiting for transfers between devices: 53.1 us -> none  [the longest x3 33.1 us: shifted(): lax.ppermute(value, axis, [(source, source + steps) for source in range(f...]
    pallas_call x0 -> x1, Pallas kernels: none -> 51.1 us  [shards(): pl.pallas_call(functools.partial(kernel, sections, count, radices, chunk)...]
    scatter-add x3 -> x0, other arithmetic: 31.5 us -> none  [tick(): spread = jnp.zeros((rows + 2 * HALO, width), jnp.float32).at[flat_ids].ad...]
    ppermute x11 -> x0, starting transfers between devices: 15 us -> none  [the longest x4 9.62 us: extended_2(): lax.ppermute(lax.slice_in_dim(block, 0, width, axis=dim), axis, backward)]
    reshape x4 -> x0, local copies, waits for them, and re-layouts: 14.3 us -> none  [the longest x3 14.2 us: tick(): jnp.broadcast_to(share[:, None, :], (rows, K, width)).reshape(-1, width)]
    broadcast_in_dim x8 -> x0, local copies, waits for them, and re-layouts: 11 us -> none  [the longest x3 7.4 us: tick(): jnp.broadcast_to(share[:, None, :], (rows, K, width)).reshape(-1, width)]
    select_n x12 -> x0, other arithmetic: 9.35 us -> none  [the longest x3 5.61 us: tick(): grads = jnp.where(valid, updated, grads)]
  transfers between devices with their start and end apart: 12 -> 0, of which waited for: 11 -> 0; matrix products, arithmetic and copies ran while one was open for 0% -> 0% of each run, Pallas kernels for 0% -> 0%
where the time goes in v1:
time: 58 us; the launch traced here: 57.7 us
  Pallas kernels  51.1 us (88%)
  local copies, waits for them, and re-layouts  5.96 us (10%)
  between operations  0.65 us (1%)
    pallas_call x1, Pallas kernels, shards(): pl.pallas_call(functools.partial(kernel, sections, count, radices, chunk)...  51.1 us
    unnamed x9, local copies, waits for them, and re-layouts  5.96 us

profile of v1, /device:TPU:0, one launch (start us, length us, event | category | flops | bytes accessed | tf_op | source)
XLA Modules:
  0.0 57.7 jit_solution(5272648835826347220)
XLA Ops:
  0.6 0.8 %copy.6.nbr = s32[128,6]{1,0:T(8,128)S(1)} copy(s32[128,6]{0,1:T(8,128)} %param.7) | data formatting | bytes 6144 | tf_op args[3]
  1.4 0.0 copy-start
  1.4 1.6 %copy-done = bf16[1,1024,1024]{2,1,0:T(8,128)(2,1)S(1)} copy-done((bf16[1,1024,1024]{2,1,0:T(8,128)(2,1)S(1)}, bf16[1,1024,1024]{2,1,0:T(8,128)(2,1)}, u32[]{:S(2)}) %copy-start) | copy-done | bytes 2097176
  3.0 0.0 copy-start.1
  3.0 1.0 %copy-done.1 = bf16[1,2,128,1024]{3,2,1,0:T(8,128)(2,1)S(1)} copy-done((bf16[1,2,128,1024]{3,2,1,0:T(8,128)(2,1)S(1)}, bf16[1,2,128,1024]{3,2,1,0:T(8,128)(2,1)}, u32[]{:S(2)}) %copy-start.1) | copy-done | bytes 524312
  4.1 0.0 copy-start.2
  4.1 1.0 %copy-done.2 = bf16[2,128,1024]{2,1,0:T(8,128)(2,1)S(1)} copy-done((bf16[2,128,1024]{2,1,0:T(8,128)(2,1)S(1)}, bf16[2,128,1024]{2,1,0:T(8,128)(2,1)}, u32[]{:S(2)}) %copy-start.2) | copy-done | bytes 524312
  5.1 51.1 %shard_map.59 = (bf16[256,1024]{1,0:T(8,128)(2,1)S(1)}, f32[64,1024]{1,0:T(8,128)S(1)}) custom-call(s32[128,6]{1,0:T(8,128)S(1)} %copy.6.nbr, bf16[2,128,1024]{2,1,0:T(8,128)(2,1)S(1)} %bitcast.6, bf16[256,1024]{1,0:T(8,128)(2,1)S(1)} %bitcast.7, bf16[1024,1024]{1,0:T(8,128)(2,1)S(1)} %bitcast.5), custom_call_target="tpu_custom_call" | custom-call | tf_op jit(solution)/shard_map/pallas_call | solution.py:306
  56.2 0.8 %copy.9 = bf16[1,2,128,1024]{3,2,1,0:T(8,128)(2,1)} copy(bf16[1,2,128,1024]{3,2,1,0:T(8,128)(2,1)S(1)} %bitcast.8) | data formatting | bytes 1048576
  57.0 0.7 %copy.10 = f32[1,64,1024]{2,1,0:T(8,128)} copy(f32[1,64,1024]{2,1,0:T(8,128)S(1)} %bitcast.9) | data formatting | bytes 524288
Async XLA Ops:
  1.4 1.6 %copy-start = (bf16[1,1024,1024]{2,1,0:T(8,128)(2,1)S(1)}, bf16[1,1024,1024]{2,1,0:T(8,128)(2,1)}, u32[]{:S(2)}) copy-start(bf16[1,1024,1024]{2,1,0:T(8,128)(2,1)} %param.6) | copy-start | bytes 6291460
  3.0 1.0 %copy-start.1 = (bf16[1,2,128,1024]{3,2,1,0:T(8,128)(2,1)S(1)}, bf16[1,2,128,1024]{3,2,1,0:T(8,128)(2,1)}, u32[]{:S(2)}) copy-start(bf16[1,2,128,1024]{3,2,1,0:T(8,128)(2,1)} %param.4) | copy-start | bytes 1572868
  4.1 1.0 %copy-start.2 = (bf16[2,128,1024]{2,1,0:T(8,128)(2,1)S(1)}, bf16[2,128,1024]{2,1,0:T(8,128)(2,1)}, u32[]{:S(2)}) copy-start(bf16[2,128,1024]{2,1,0:T(8,128)(2,1)} %param.5) | copy-start | bytes 1572868

commit v2 on v1

--- a/solution.py
+++ b/solution.py
@@ -22,7 +22,7 @@
             found.append(2)
             count //= 2
     while count > 1:
-        factor = next(f for f in (2, 3, 5, 7, count) if count % f == 0)
+        factor = next(f for f in (4, 2, 3, 5, 7, count) if count % f == 0)
         found.append(factor)
         count //= factor
     return tuple(found)
@@ -40,8 +40,8 @@
     return place
 
 
-def kernel(sections, count, radices, chunk, nbr, acts, ups_hbm, w_hbm, out, wgrad, *scratch):
-    (w, ups, acts_lo, acts_hi, nbr_lo, nbr_hi, z, zt, fac, g_in, g_out, du, du_lo, du_hi, e,
+def kernel(sections, count, radices, chunk, nbr, acts_hbm, ups_hbm, w_hbm, out, wgrad, *scratch):
+    (w, ups, acts, acts_lo, acts_hi, nbr_lo, nbr_hi, z, zt, fac, g_in, g_out, du, du_lo, du_hi, e,
      load_sem, acts_send, acts_recv, nbr_send, nbr_recv, g_send, g_recv, du_send, du_recv,
      rs_send, rs_recv, *rs) = scratch
     stages = len(radices)
@@ -66,6 +66,8 @@
 
     loads = [pltpu.make_async_copy(w_hbm, w, load_sem.at[0]),
              pltpu.make_async_copy(ups_hbm, ups, load_sem.at[1])]
+    load_acts = pltpu.make_async_copy(acts_hbm, acts, load_sem.at[2])
+    load_acts.start()
     for copy in loads:
         copy.start()
 
@@ -92,34 +94,31 @@
 
     first, last = pl.ds(0, HALO), pl.ds(rows - HALO, HALO)
     halos = [
-        remote(acts.at[:, last], acts_lo, acts_send.at[0], acts_recv.at[0], (s, right)),
-        remote(acts.at[:, first], acts_hi, acts_send.at[1], acts_recv.at[1], (s, left)),
-        remote(nbr.at[last], nbr_lo, nbr_send.at[0], nbr_recv.at[0], (s, right)),
-        remote(nbr.at[first], nbr_hi, nbr_send.at[1], nbr_recv.at[1], (s, left)),
+        remote(acts_hbm.at[:, last], acts_lo, acts_send.at[0], acts_recv.at[0], (s, right)),
+        remote(acts_hbm.at[:, first], acts_hi, acts_send.at[1], acts_recv.at[1], (s, left)),
+        remote(nbr, nbr_lo, nbr_send.at[0], nbr_recv.at[0], (s, right)),
+        remote(nbr, nbr_hi, nbr_send.at[1], nbr_recv.at[1], (s, left)),
     ]
     for copy in halos:
         copy.start()
 
     total = rows * count
 
-    def counts(ids, shift, lanes):
+    def counts(ids, shift, places):
         local = ids - me * rows + shift
         local = jnp.where(local < 0, local + total, local)
         local = jnp.where(local >= total, local - total, local)
-        places = lax.broadcasted_iota(jnp.int32, (ids.shape[0], lanes), 1)
-        found = jnp.zeros(places.shape, F32)
+        place = lax.broadcasted_iota(jnp.int32, (places, ids.shape[1]), 0)
+        found = jnp.zeros(place.shape, F32)
         for k in range(K):
-            found = found + jnp.where(local[:, k:k + 1] == places, 1.0, 0.0)
-        return found.astype(BF16)
-
-    gather = counts(nbr[...], HALO, span)
+            found = found + jnp.where(local[k:k + 1] == place, 1.0, 0.0)
+        return found
+
+    gather = counts(nbr[...], HALO, span).T.astype(BF16)
     own = counts(nbr[...], 0, rows)
-
-    for copy in halos:
+    load_acts.wait()
+    for copy in halos[:2]:
         copy.wait_recv()
-    scatter = jnp.concatenate(
-        [counts(nbr_lo[...], 0, rows), own, counts(nbr_hi[...], 0, rows)], axis=0
-    ).astype(F32).T.astype(BF16)
 
     for m in range(micro):
         field = jnp.concatenate([acts_lo[m], acts[m], acts_hi[m]], axis=0)
@@ -127,6 +126,15 @@
         z[m * rows:(m + 1) * rows] = (acts[m].astype(F32) + agg).astype(BF16)
     for copy in loads:
         copy.wait()
+    for copy in halos[2:]:
+        copy.wait_recv()
+    lane = lax.broadcasted_iota(jnp.int32, nbr.shape, 1)
+    beside = jnp.where(lane < HALO, nbr_hi[...], nbr_lo[...])
+    beside = counts(beside, 0, rows)
+    inner = lax.broadcasted_iota(jnp.int32, beside.shape, 1)
+    edge = jnp.logical_or(inner < HALO, inner >= rows - HALO)
+    scatter = jnp.concatenate([own, jnp.where(edge, beside, 0.0)], axis=1).astype(BF16)
+    blank = jnp.zeros((rows - 2 * HALO, chunk), BF16)
 
     def columns(c):
         return slice(c * chunk, (c + 1) * chunk)
@@ -156,7 +164,7 @@
         for copy in du_copies(c):
             copy.wait_recv()
         for m in range(micro):
-            field = jnp.concatenate([du_lo[c, m], du[c, m], du_hi[c, m]], axis=0)
+            field = jnp.concatenate([du[c, m], du_hi[c, m], blank, du_lo[c, m]], axis=0)
             spread = jnp.dot(scatter, field, preferred_element_type=F32) * (1.0 / K)
             e[m * rows:(m + 1) * rows, columns(c)] = (du[c, m].astype(F32) + spread).astype(BF16)
 
@@ -217,13 +225,13 @@
             put_du(c, ups[:, columns(c)].astype(F32) * factor(c))
         turn()
         for c in range(chunks):
-            weight_part(c)
-        for c in range(chunks):
             mix(c)
         for c in range(chunks):
             g_out[c] = cotangent(c, ups[:, columns(c)])
             if sections > 1:
                 g_copy(c).start()
+        for c in range(chunks):
+            weight_part(c)
         for step in range(chunks + stages - 1):
             rs_wave(step)
         if sections > 1:
@@ -240,9 +248,9 @@
                 g_copy(c).wait_recv()
                 put_du(c, g_in[c].astype(F32) * fac[:, columns(c)])
                 weight_part(c)
-                if c:
-                    rs_wave(c - 1)
-            rs_wave(chunks - 1)
+                for t in reversed(range(stages)):
+                    if 0 <= c - t:
+                        rs_step(t, c - t)
             for c in range(chunks):
                 mix(c)
             for c in range(chunks):
@@ -286,10 +294,11 @@
     scratch = [
         pltpu.VMEM((width, width), BF16),
         pltpu.VMEM((tall, width), BF16),
+        pltpu.VMEM((micro, rows, width), BF16),
         pltpu.VMEM((micro, HALO, width), BF16),
         pltpu.VMEM((micro, HALO, width), BF16),
-        pltpu.VMEM((HALO, K), jnp.int32),
-        pltpu.VMEM((HALO, K), jnp.int32),
+        pltpu.VMEM((K, rows), jnp.int32),
+        pltpu.VMEM((K, rows), jnp.int32),
         pltpu.VMEM((tall, width), BF16),
         pltpu.VMEM((width, tall), BF16),
         pltpu.VMEM((tall, width), F32),
@@ -299,7 +308,7 @@
         pltpu.VMEM((chunks, micro, HALO, chunk), BF16),
         pltpu.VMEM((chunks, micro, HALO, chunk), BF16),
         pltpu.VMEM((tall, width), BF16),
-        dma((2,)), dma((2,)), dma((2,)), dma((2,)), dma((2,)), dma((chunks,)), dma((chunks,)),
+        dma((3,)), dma((2,)), dma((2,)), dma((2,)), dma((2,)), dma((chunks,)), dma((chunks,)),
         dma((2 * chunks,)), dma((2 * chunks,)), dma((flights,)), dma((flights,)),
     ] + parts + landed
     vmem = pl.BlockSpec(memory_space=pltpu.VMEM)
@@ -309,12 +318,12 @@
             jax.ShapeDtypeStruct((tall, width), BF16),
             jax.ShapeDtypeStruct((deep, width), F32),
         ),
-        in_specs=[vmem, vmem, pl.BlockSpec(memory_space=pl.ANY), pl.BlockSpec(memory_space=pl.ANY)],
+        in_specs=[vmem, pl.BlockSpec(memory_space=pl.ANY), pl.BlockSpec(memory_space=pl.ANY), pl.BlockSpec(memory_space=pl.ANY)],
         out_specs=(vmem, vmem),
         scratch_shapes=scratch,
         compiler_params=pltpu.CompilerParams(
-            collective_id=0, has_side_effects=True, vmem_limit_bytes=48 * 1024 * 1024),
-    )(neighbours, acts[0], upstream.reshape(tall, width), weights[0])
+            collective_id=0, has_side_effects=True, vmem_limit_bytes=60 * 1024 * 1024),
+    )(neighbours.T, acts[0], upstream.reshape(tall, width), weights[0])
     return grads.reshape(1, micro, rows, width), weight_grad[None]
 
 

time: 58 us -> 53.6 us (0.924)
  local copies, waits for them, and re-layouts: 5.96 us -> 3.54 us
  Pallas kernels: 51.1 us -> 49.2 us
    unnamed x9 -> x2, local copies, waits for them, and re-layouts: 5.96 us -> 3.54 us
    pallas_call x1, Pallas kernels: 51.1 us -> 49.2 us  [shards(): pl.pallas_call(functools.partial(kernel, sections, count, radices, chunk)...]
where the time goes in v2:
time: 53.6 us; the launch traced here: 53.4 us
  Pallas kernels  49.2 us (92%)
  local copies, waits for them, and re-layouts  3.54 us (7%)
  between operations  0.64 us (1%)
    pallas_call x1, Pallas kernels, shards(): pl.pallas_call(functools.partial(kernel, sections, count, radices, chunk)...  49.2 us
    unnamed x2, local copies, waits for them, and re-layouts  3.54 us

profile of v2, /device:TPU:0, one launch (start us, length us, event | category | flops | bytes accessed | tf_op | source)
XLA Modules:
  0.0 53.4 jit_solution(8679628247226606163)
XLA Ops:
  0.6 49.2 %shard_map.59 = (bf16[256,1024]{1,0:T(8,128)(2,1)}, f32[64,1024]{1,0:T(8,128)}) custom-call(s32[6,128]{1,0:T(8,128)} %bitcast.11, bf16[2,128,1024]{2,1,0:T(8,128)(2,1)} %bitcast.8, bf16[256,1024]{1,0:T(8,128)(2,1)} %bitcast.9, bf16[1024,1024]{1,0:T(8,128)(2,1)} %bitcast.6), custom_call_target="tpu_custom_call" | custom-call | tf_op jit(solution)/shard_map/pallas_call | solution.py:315
  49.9 1.9 %copy.8 = bf16[1,2,128,1024]{3,2,1,0:T(8,128)(2,1)} copy(bf16[1,2,128,1024]{3,2,1,0:T(8,128)(2,1)} %bitcast.7) | data formatting | bytes 1048576
  51.7 1.7 %copy.9 = f32[1,64,1024]{2,1,0:T(8,128)} copy(f32[1,64,1024]{2,1,0:T(8,128)} %bitcast.10) | data formatting | bytes 524288

commit v3 on v2

--- a/solution.py
+++ b/solution.py
@@ -248,9 +248,8 @@
                 g_copy(c).wait_recv()
                 put_du(c, g_in[c].astype(F32) * fac[:, columns(c)])
                 weight_part(c)
-                for t in reversed(range(stages)):
-                    if 0 <= c - t:
-                        rs_step(t, c - t)
+                for t in range(min(stages, c + 1)):
+                    rs_step(t, c - t)
             for c in range(chunks):
                 mix(c)
             for c in range(chunks):

time: 53.6 us -> 51.2 us (0.955)
  Pallas kernels: 49.2 us -> 46.8 us
    pallas_call x1, Pallas kernels: 49.2 us -> 46.8 us  [shards(): pl.pallas_call(functools.partial(kernel, sections, count, radices, chunk)...]
where the time goes in v3:
time: 51.2 us; the launch traced here: 51 us
  Pallas kernels  46.8 us (91%)
  local copies, waits for them, and re-layouts  3.54 us (7%)
  between operations  0.64 us (1%)
    pallas_call x1, Pallas kernels, shards(): pl.pallas_call(functools.partial(kernel, sections, count, radices, chunk)...  46.8 us
    unnamed x2, local copies, waits for them, and re-layouts  3.54 us

profile of v3, /device:TPU:0, one launch (start us, length us, event | category | flops | bytes accessed | tf_op | source)
XLA Modules:
  0.0 51.0 jit_solution(17522736225512319860)
XLA Ops:
  0.6 46.8 %shard_map.59 = (bf16[256,1024]{1,0:T(8,128)(2,1)}, f32[64,1024]{1,0:T(8,128)}) custom-call(s32[6,128]{1,0:T(8,128)} %bitcast.11, bf16[2,128,1024]{2,1,0:T(8,128)(2,1)} %bitcast.8, bf16[256,1024]{1,0:T(8,128)(2,1)} %bitcast.9, bf16[1024,1024]{1,0:T(8,128)(2,1)} %bitcast.6), custom_call_target="tpu_custom_call" | custom-call | tf_op jit(solution)/shard_map/pallas_call | solution.py:314
  47.4 1.9 %copy.8 = bf16[1,2,128,1024]{3,2,1,0:T(8,128)(2,1)} copy(bf16[1,2,128,1024]{3,2,1,0:T(8,128)(2,1)} %bitcast.7) | data formatting | bytes 1048576
  49.3 1.7 %copy.9 = f32[1,64,1024]{2,1,0:T(8,128)} copy(f32[1,64,1024]{2,1,0:T(8,128)} %bitcast.10) | data formatting | bytes 524288
